TPU v7x, 32 devices: a whole 2x2x4 slice. The times are simulated.
32 devices in a mesh: grp: 2 (over x), grid: 16 (over z, y, core).
Axes of the slice: x: 2, y: 2, z: 4, core: 2. Of those that a mesh axis runs over, the one named last changes fastest.
Arguments:
- valence: bfloat16 [32768, 48], P(('grp', 'grid')), parts along dimension 0, may hold values from -24 to 24
- conduction: bfloat16 [32768, 512], P(('grp', 'grid')), parts along dimension 0, may hold values from -6 to 6
- potentials: bfloat16 [32768, 64], P(('grp', 'grid')), parts along dimension 0, may hold values from -6 to 6
- eigenpotentials: bfloat16 [32768, 1024], P(('grp', 'grid')), parts along dimension 0, may hold values from -0.1875 to 0.1875
- valence_energy: float32 [96], P('grp'), parts along dimension 0, may hold values from -6 to -1
- conduction_energy: float32 [1024], P('grp'), parts along dimension 0, may hold values from 0.5 to 20
Outputs:
- projected: float32 [2048, 64], P(('grp', 'grid')), parts along dimension 0
- complementary: float32 [32768, 64], P(('grp', 'grid')), parts along dimension 0
There are 2 independent parts, one for each index of `grp`. A program takes and returns all parts, laid end to end along the dimension named above; each array names one. Nothing has to cross between parts.
All inputs are finite; a program needn't handle non-finite values.
Results may differ from a plain program's by a relative error of at most 0.0042.
Values may be sent and summed in bfloat16 or wider, within the bound.
A program may use at most 64 MiB of HBM per device.

v0:
```python
import jax
import jax.numpy as jnp
from jax import lax
from jax.sharding import PartitionSpec as P


def contract_rows(left, right):
    return lax.dot_general(
        left, right, (((0,), (0,)), ((), ())), preferred_element_type=jnp.float32
    )


def body(valence, conduction, potentials, eigenpotentials, valence_energy, conduction_energy):
    grid_rows = valence.shape[0]
    valence_count = valence.shape[1]
    conduction_count = conduction.shape[1]
    potential_count = potentials.shape[1]
    eigen_count = eigenpotentials.shape[1]
    devices_grid = lax.axis_size("grid")
    points_total = grid_rows * devices_grid
    pair_count = potential_count * valence_count
    joined = potentials.astype(jnp.float32)[:, :, None] * valence.astype(jnp.float32)[:, None, :]
    paired = joined.reshape(grid_rows, pair_count).astype(jnp.bfloat16)
    coefficients = lax.psum(contract_rows(conduction, paired), "grid")
    denominators = valence_energy[None, :] - conduction_energy[:, None]
    shaped = coefficients.reshape(conduction_count, potential_count, valence_count)
    scaled = (
        (shaped * (4.0 / points_total) / denominators[:, None, :])
        .reshape(conduction_count, pair_count)
        .astype(jnp.bfloat16)
    )
    combined = jnp.dot(conduction, scaled, preferred_element_type=jnp.float32)
    response = jnp.sum(
        combined.reshape(grid_rows, potential_count, valence_count)
        * valence.astype(jnp.float32)[:, None, :],
        axis=2,
    )
    response_low = response.astype(jnp.bfloat16)
    eigen_block = eigenpotentials
    intersection_share = lax.psum_scatter(
        contract_rows(eigen_block, response_low), "grid", scatter_dimension=0, tiled=True
    )
    squares = lax.psum(jnp.sum(intersection_share * intersection_share, axis=0), "grid")
    projected = intersection_share / jnp.sqrt(squares / eigen_count + 1e-06)
    eigen_block = eigenpotentials
    back_part = jnp.dot(
        eigen_block,
        lax.all_gather(intersection_share.astype(jnp.bfloat16), "grid", axis=0, tiled=True),
        preferred_element_type=jnp.float32,
    )
    remainder = response - back_part
    remainder_sq = lax.psum(jnp.sum(remainder * remainder, axis=0), "grid")
    complementary = remainder / jnp.sqrt(remainder_sq / points_total + 1e-06)
    return (projected, complementary)


def solution(mesh):
    return jax.shard_map(
        body,
        mesh=mesh,
        in_specs=(
            P(("grp", "grid"), None),
            P(("grp", "grid"), None),
            P(("grp", "grid"), None),
            P(("grp", "grid"), None),
            P("grp"),
            P("grp"),
        ),
        out_specs=(P(("grp", "grid"), None), P(("grp", "grid"), None)),
        check_vma=False,
    )
```

profile of v0, /device:TPU:0, one launch (start us, length us, event | category | flops | bytes accessed | tf_op | source)
XLA Modules:
  0.0 285.6 jit_solution(762597081157384395)
XLA Ops:
  7.2 0.0 copy-start
  7.2 0.0 copy-start.3
  7.2 0.0 all-reduce.3.cloned.1.call-start
  7.2 1.1 convert_element_type.23
  8.3 0.9 convert_element_type.22
  9.3 2.1 multiply_convert_fusion
  11.4 0.0 copy-done.3
  11.4 5.3 %convolution_bitcast_fusion = f32[512,3072]{0,1:T(8,128)} fusion(bf16[1024,3072]{0,1:T(8,128)(2,1)S(1)} %bitcast.25, bf16[1024,512]{1,0:T(8,128)(2,1)S(1)} %copy-done.3), kind=kOutput, calls=%fused_computation.4 | convolution fusion | flops 3221225472 | bytes 13631488 | tf_op jit(solution)/shard_map/dot_general | solution.py:8
  16.7 0.0 copy-start.1
  16.7 0.0 copy-start.2
  16.7 0.0 all-reduce.3.cloned.1.call-update
  16.7 0.0 reduce-scatter.4.cloned.1.call-start
  16.8 0.6 copy-done.1
  17.4 0.0 copy-done.2
  17.4 0.1 broadcast_subtract_fusion
  17.4 141.2 %all-reduce.3.cloned.1.call-done = f32[512,3072]{0,1:T(8,128)} async-done(((f32[512,3072]{0,1:T(8,128)}), f32[512,3072]{0,1:T(8,128)}) %all-reduce.3.cloned.1.call-update) | async-done | bytes 6291472 | tf_op jit(solution)/shard_map/psum | solution.py:24
  158.6 3.7 %fusion = bf16[512,3072]{0,1:T(8,128)(2,1)S(1)} fusion(f32[512,3072]{0,1:T(8,128)} %all-reduce.3.cloned.1.call-done, f32[512,48]{0,1:T(8,128)S(1)} %broadcast_subtract_fusion), kind=kLoop, calls=%fused_computation.3 | loop fusion | flops 4718592 | bytes 9535488 | tf_op jit(solution)/shard_map/convert_element_type | solution.py:30
  162.3 3.5 %fusion.4 = f32[3072,1024]{1,0:T(8,128)S(1)} fusion(bf16[512,3072]{0,1:T(8,128)(2,1)S(1)} %fusion, bf16[1024,512]{1,0:T(8,128)(2,1)S(1)} %copy-done.3), kind=kOutput, calls=%fused_computation.17 | convolution fusion | flops 3221225472 | bytes 16777216 | tf_op jit(solution)/shard_map/dot_general | solution.py:32
  165.7 2.1 multiply_reduce_fusion
  167.8 0.0 copy-done
  167.8 0.5 convolution_bitcast_fusion.2
  168.3 1.0 copy.11
  169.3 0.0 reduce-scatter.4.cloned.1.call-update
  169.4 56.0 %reduce-scatter.4.cloned.1.call-done = f32[64,64]{1,0:T(8,128)} async-done(((f32[1024,64]{1,0:T(8,128)}), f32[64,64]{1,0:T(8,128)}) %reduce-scatter.4.cloned.1.call-update) | async-done | bytes 16400
  225.3 0.8 copy.12
  226.2 0.1 fusion.3
  226.3 0.1 copy.9
  226.4 20.1 %all_gather.3 = bf16[1024,64]{1,0:T(8,128)(2,1)S(1)} all-gather(bf16[64,64]{1,0:T(8,128)(2,1)S(1)} %copy.9), channel_id=1, replica_groups=mesh['grp'=2,'grid'=16] {'grid'}, dimensions={0}, use_global_device_ids=true | all-gather | bytes 139264 | tf_op jit(solution)/shard_map/all_gather | solution.py:48
  246.5 0.9 multiply_reduce_fusion.1
  247.4 29.8 %all-reduce = (f32[64]{0:T(128)S(1)}, f32[64]{0:T(128)S(1)}) all-reduce(f32[64]{0:T(128)S(1)} %get-tuple-element.9, f32[64]{0:T(128)S(1)} %get-tuple-element.10), channel_id=1, replica_groups=mesh['grp'=2,'grid'=16] {'grid'}, use_global_device_ids=true, to_apply=%region_4.0 | all-reduce | flops 128 | bytes 1024 | tf_op jit(solution)/shard_map/psum | solution.py:43
  277.2 0.1 broadcast_divide_fusion.1
  277.3 0.7 copy.10
  278.0 0.8 broadcast_divide_fusion
  (1 shorter events, 0.0 us)
Async XLA Ops:
  7.2 160.7 %copy-start = (bf16[1024,1024]{1,0:T(8,128)(2,1)S(1)}, bf16[1024,1024]{1,0:T(8,128)(2,1)}, u32[]{:S(2)}) copy-start(bf16[1024,1024]{1,0:T(8,128)(2,1)} %param.9) | copy-start | bytes 6291460
  7.2 4.2 %copy-start.3 = (bf16[1024,512]{1,0:T(8,128)(2,1)S(1)}, bf16[1024,512]{1,0:T(8,128)(2,1)}, u32[]{:S(2)}) copy-start(bf16[1024,512]{1,0:T(8,128)(2,1)} %param.7) | copy-start | bytes 3145732
  7.2 151.4 %all-reduce.3.cloned.1.call-start = ((), (), s32[]{:S(2)}) async-start(), calls=%async_computation.1 | async-start | bytes 12582912 | tf_op jit(solution)/shard_map/psum | solution.py:24
  16.7 0.7 copy-start.1
  16.7 0.7 copy-start.2
  16.7 208.6 %reduce-scatter.4.cloned.1.call-start = ((), (), s32[]{:S(2)}) async-start(), calls=%async_computation.2 | async-start | bytes 557056
Sparse Core Ops, SparseCore 0:
  16.8 141.7 all-reduce.2
  169.5 55.8 reduce-scatter.3
where the time goes:
time: 286 us
  waiting for transfers between devices  197 us (69%)
  blocking collectives  50 us (17%)
  between operations  14.1 us (5%)
  other arithmetic  11 us (4%)
  matrix products  10.1 us (4%)
  local copies, waits for them, and re-layouts  3.24 us (1%)
    psum x1, waiting for transfers between devices, body(): coefficients = lax.psum(contract_rows(conduction, paired), 'grid')  141 us
    unnamed x3, waiting for transfers between devices  56 us
    psum x1, blocking collectives, body(): lax.psum(jnp.sum(intersection_share * intersection_share, axis=0), 'grid')  29.8 us
    all_gather x1, blocking collectives, body(): lax.all_gather(intersection_share.astype(jnp.bfloat16), 'grid', axis=0, t...  20.1 us
    dot_general x2, matrix products, contract_rows(): lax.dot_general(left, right, (((0,), (0,)), ((), ())), preferred_element_...  5.77 us
  transfers between devices with their start and end apart: 2, of which 2 were waited for; matrix products, arithmetic and copies ran while one was open for 0% of the time, Pallas kernels for 0%

commit v1 on v0

v1 whole, which is shorter than its diff:
```python
import functools

import jax
import jax.numpy as jnp
from jax import lax
from jax.experimental import pallas as pl
from jax.experimental.pallas import tpu as pltpu
from jax.sharding import PartitionSpec as P

MESH = pl.DeviceIdType.MESH
VMEM_BYTES = 56 * 1024 * 1024


def contract_rows(left, right):
    return lax.dot_general(
        left, right, (((0,), (0,)), ((), ())), preferred_element_type=jnp.float32
    )


def bit_of(me, bit):
    return lax.rem(lax.div(me, 1 << bit), 2)


def partner_of(me, bit):
    return me + (1 - 2 * bit_of(me, bit)) * (1 << bit)


def aligned(row, step):
    return pl.multiple_of(row, step)


def reversed_bits(value, bits):
    return sum(((value >> b) & 1) << (bits - 1 - b) for b in range(bits))


def couple_kernel(n, orders, part_ref, weight_ref, out_ref, acc, sent, got, send_sem, recv_sem):
    levels = n.bit_length() - 1
    me = lax.axis_index("grid")
    rows, columns = part_ref.shape
    unit = weight_ref.shape[0]
    block = rows // n
    width = columns // len(orders)

    barrier = pltpu.get_barrier_semaphore()
    for bit in range(levels):
        pl.semaphore_signal(
            barrier, inc=1, device_id={"grid": partner_of(me, bit)}, device_id_type=MESH
        )
    pl.semaphore_wait(barrier, levels)

    slots = [rows - (rows >> s) for s in range(levels)]
    bases = [[0] for _ in orders]
    copies = [[] for _ in orders]

    for s in range(levels + 1):
        for q, order in enumerate(orders):
            cols = pl.ds(q * width, width)
            base = bases[q][s]
            source = part_ref if s <= 1 else acc
            if s > 0:
                copies[q][s - 1].wait_recv()

            def term(row, offset, s=s, source=source, cols=cols):
                value = source[pl.ds(aligned(row + offset, unit), unit), cols]
                if s > 0:
                    value = value + got[
                        pl.ds(aligned(slots[s - 1] + offset, unit), unit), cols
                    ].astype(jnp.float32)
                return value

            if s == levels:
                def finish(i, _, term=term, base=base, cols=cols):
                    scaled = term(base * block, i * unit) * weight_ref[:, cols]
                    out_ref[pl.ds(aligned(base * block + i * unit, unit), unit), cols] = (
                        scaled.astype(jnp.bfloat16)
                    )
                    return 0

                lax.fori_loop(0, block // unit, finish, 0)
                continue
            half = n >> (s + 1)
            bit = bit_of(me, order[s])
            leave, keep = (1 - bit) * half * block, bit * half * block

            def pack(i, _, term=term, base=base, leave=leave, s=s, cols=cols):
                sent[pl.ds(aligned(slots[s] + i * unit, unit), unit), cols] = term(
                    base * block, leave + i * unit
                ).astype(jnp.bfloat16)
                return 0

            lax.fori_loop(0, half * block // unit, pack, 0)
            copy = pltpu.make_async_remote_copy(
                src_ref=sent.at[pl.ds(slots[s], half * block), cols],
                dst_ref=got.at[pl.ds(slots[s], half * block), cols],
                send_sem=send_sem.at[q, s],
                recv_sem=recv_sem.at[q, s],
                device_id={"grid": partner_of(me, order[s])},
                device_id_type=MESH,
            )
            copy.start()
            copies[q].append(copy)
            if s > 0:
                def add(i, _, term=term, base=base, keep=keep, cols=cols):
                    acc[pl.ds(aligned(base * block + keep + i * unit, unit), unit), cols] = term(
                        base * block, keep + i * unit
                    )
                    return 0

                lax.fori_loop(0, half * block // unit, add, 0)
            bases[q].append(base + bit * half)

    for s in reversed(range(levels)):
        for q, order in enumerate(orders):
            if s < levels - 1:
                copies[q][-1].wait_recv()
            size = (n >> (s + 1)) * block
            view = out_ref.at[
                pl.ds(aligned(bases[q][s + 1] * block, unit), size), pl.ds(q * width, width)
            ]
            copy = pltpu.make_async_remote_copy(
                src_ref=view,
                dst_ref=view,
                send_sem=send_sem.at[q, 2 * levels - 1 - s],
                recv_sem=recv_sem.at[q, 2 * levels - 1 - s],
                device_id={"grid": partner_of(me, order[s])},
                device_id_type=MESH,
            )
            copy.start()
            copies[q].append(copy)
    for q in range(len(orders)):
        copies[q][-1].wait_recv()
        for copy in copies[q]:
            copy.wait_send()


def project_kernel(
    n, eigen_ref, response_ref, projected_ref, complementary_ref,
    acc, got, gathered, low, sums, send_sem, recv_sem, sum_send, sum_recv,
):
    levels = n.bit_length() - 1
    me = lax.axis_index("grid")
    points, eigens = eigen_ref.shape
    block = eigens // n

    barrier = pltpu.get_barrier_semaphore()
    for offset in range(1, n):
        pl.semaphore_signal(
            barrier, inc=1, device_id={"grid": lax.rem(me + offset, n)}, device_id_type=MESH
        )

    response_low = response_ref[...].astype(jnp.bfloat16)
    strip = min(256, eigens)
    for start in range(0, eigens, strip):
        strip_sum = contract_rows(eigen_ref[:, start:start + strip], response_low)
        for b in range(strip // block):
            place = reversed_bits(start // block + b, levels) * block
            acc[place:place + block, :] = strip_sum[b * block:(b + 1) * block, :]
    pl.semaphore_wait(barrier, n - 1)

    slots = [eigens - (eigens >> s) for s in range(levels)]
    bases = [0]
    copies = []
    for s in range(levels):
        half = n >> (s + 1)
        bit = bit_of(me, s)
        leave = (bases[s] + (1 - bit) * half) * block
        keep = (bases[s] + bit * half) * block
        copy = pltpu.make_async_remote_copy(
            src_ref=acc.at[pl.ds(aligned(leave, block), half * block)],
            dst_ref=got.at[pl.ds(slots[s], half * block)],
            send_sem=send_sem.at[s],
            recv_sem=recv_sem.at[s],
            device_id={"grid": partner_of(me, s)},
            device_id_type=MESH,
        )
        copy.start()
        copies.append(copy)
        copy.wait_recv()
        kept = pl.ds(aligned(keep, block), half * block)
        acc[kept, :] = acc[kept, :] + got[pl.ds(slots[s], half * block), :]
        bases.append(bases[s] + bit * half)

    own = pl.ds(aligned(bases[levels] * block, block), block)
    mine = acc[own, :]
    gathered[own, :] = mine.astype(jnp.bfloat16)
    for s in reversed(range(levels)):
        view = gathered.at[pl.ds(aligned(bases[s + 1] * block, block), (n >> (s + 1)) * block)]
        copy = pltpu.make_async_remote_copy(
            src_ref=view,
            dst_ref=view,
            send_sem=send_sem.at[2 * levels - 1 - s],
            recv_sem=recv_sem.at[2 * levels - 1 - s],
            device_id={"grid": partner_of(me, s)},
            device_id_type=MESH,
        )
        copy.start()
        copies.append(copy)
        copy.wait_recv()
    for b in range(n):
        place = reversed_bits(b, levels) * block
        low[b * block:(b + 1) * block, :] = gathered[place:place + block, :]

    intersection_low = low[...]
    remainder = response_ref[...] - jnp.dot(
        eigen_ref[...], intersection_low, preferred_element_type=jnp.float32
    )
    sums[me] = jnp.broadcast_to(
        jnp.sum(remainder * remainder, axis=0, keepdims=True), sums.shape[1:]
    )
    for offset in range(1, n):
        copy = pltpu.make_async_remote_copy(
            src_ref=sums.at[me],
            dst_ref=sums.at[me],
            send_sem=sum_send.at[offset],
            recv_sem=sum_recv.at[offset],
            device_id={"grid": lax.rem(me + offset, n)},
            device_id_type=MESH,
        )
        copy.start()
        copies.append(copy)
    complementary_ref[...] = remainder
    wide = intersection_low.astype(jnp.float32)
    squares = jnp.sum(wide * wide, axis=0, keepdims=True)
    projected_ref[...] = mine / jnp.sqrt(squares / eigens + 1e-06)
    for offset in range(1, n):
        other = lax.rem(me + n - offset, n)
        pltpu.make_async_remote_copy(
            src_ref=sums.at[other],
            dst_ref=sums.at[other],
            send_sem=sum_send.at[offset],
            recv_sem=sum_recv.at[offset],
            device_id={"grid": other},
            device_id_type=MESH,
        ).wait_recv()
    total = jnp.sum(sums[...], axis=0)[0:1, :]
    complementary_ref[...] = complementary_ref[...] / jnp.sqrt(total / (points * n) + 1e-06)
    for copy in copies:
        copy.wait_send()


def body(valence, conduction, potentials, eigenpotentials, valence_energy, conduction_energy):
    grid_rows = valence.shape[0]
    valence_count = valence.shape[1]
    conduction_count = conduction.shape[1]
    potential_count = potentials.shape[1]
    eigen_count = eigenpotentials.shape[1]
    n = lax.axis_size("grid")
    levels = n.bit_length() - 1
    points_total = grid_rows * n
    pair_count = potential_count * valence_count
    vmem = pl.BlockSpec(memory_space=pltpu.VMEM)

    joined = potentials.astype(jnp.float32)[:, :, None] * valence.astype(jnp.float32)[:, None, :]
    paired = joined.reshape(grid_rows, pair_count).astype(jnp.bfloat16)
    partial = contract_rows(paired, conduction)
    weight = (4.0 / points_total) / (valence_energy[:, None] - conduction_energy[None, :])

    plain = list(range(levels))
    crossed = [0, 2, 1] + plain[3:] if levels >= 3 else plain
    orders = [plain, crossed] * (conduction_count // 256)
    shape = (pair_count, conduction_count)
    scaled = pl.pallas_call(
        functools.partial(couple_kernel, n, orders),
        out_shape=jax.ShapeDtypeStruct(shape, jnp.bfloat16),
        in_specs=[vmem] * 2,
        out_specs=vmem,
        scratch_shapes=[
            pltpu.VMEM(shape, jnp.float32),
            pltpu.VMEM(shape, jnp.bfloat16),
            pltpu.VMEM(shape, jnp.bfloat16),
            pltpu.SemaphoreType.DMA((len(orders), 2 * levels)),
            pltpu.SemaphoreType.DMA((len(orders), 2 * levels)),
        ],
        compiler_params=pltpu.CompilerParams(
            collective_id=0, has_side_effects=True, vmem_limit_bytes=VMEM_BYTES
        ),
    )(partial, weight)

    combined = lax.dot_general(
        conduction, scaled, (((1,), (1,)), ((), ())), preferred_element_type=jnp.float32
    )
    response = jnp.sum(
        combined.reshape(grid_rows, potential_count, valence_count)
        * valence.astype(jnp.float32)[:, None, :],
        axis=2,
    )

    return pl.pallas_call(
        functools.partial(project_kernel, n),
        out_shape=(
            jax.ShapeDtypeStruct((eigen_count // n, potential_count), jnp.float32),
            jax.ShapeDtypeStruct((grid_rows, potential_count), jnp.float32),
        ),
        in_specs=[vmem] * 2,
        out_specs=(vmem, vmem),
        scratch_shapes=[
            pltpu.VMEM((eigen_count, potential_count), jnp.float32),
            pltpu.VMEM((eigen_count, potential_count), jnp.float32),
            pltpu.VMEM((eigen_count, potential_count), jnp.bfloat16),
            pltpu.VMEM((eigen_count, potential_count), jnp.bfloat16),
            pltpu.VMEM((n, 8, potential_count), jnp.float32),
            pltpu.SemaphoreType.DMA((2 * levels,)),
            pltpu.SemaphoreType.DMA((2 * levels,)),
            pltpu.SemaphoreType.DMA((n,)),
            pltpu.SemaphoreType.DMA((n,)),
        ],
        compiler_params=pltpu.CompilerParams(
            collective_id=1, has_side_effects=True, vmem_limit_bytes=VMEM_BYTES
        ),
    )(eigenpotentials, response)


def solution(mesh):
    return jax.shard_map(
        body,
        mesh=mesh,
        in_specs=(
            P(("grp", "grid"), None),
            P(("grp", "grid"), None),
            P(("grp", "grid"), None),
            P(("grp", "grid"), None),
            P("grp"),
            P("grp"),
        ),
        out_specs=(P(("grp", "grid"), None), P(("grp", "grid"), None)),
        check_vma=False,
    )
```

time: 286 us -> 115 us (0.40)
  waiting for transfers between devices: 197 us -> 0 us
  Pallas kernels: 0 us -> 91.1 us
  blocking collectives: 50 us -> 0 us
  between operations: 14.1 us -> 0.69 us
  other arithmetic: 11 us -> 7.56 us
    psum x1 -> x0, waiting for transfers between devices: 141 us -> none  [body(): coefficients = lax.psum(contract_rows(conduction, paired), 'grid')]
    pallas_call x0 -> x2, Pallas kernels: none -> 91.1 us  [the longest x1 56.7 us: body(): pl.pallas_call(functools.partial(couple_kernel, n, orders), out_shape=jax...]
    unnamed x3 -> x0, waiting for transfers between devices: 56 us -> none
    psum x1 -> x0, blocking collectives: 29.8 us -> none  [body(): lax.psum(jnp.sum(intersection_share * intersection_share, axis=0), 'grid')]
    all_gather x1 -> x0, blocking collectives: 20.1 us -> none  [body(): lax.all_gather(intersection_share.astype(jnp.bfloat16), 'grid', axis=0, t...]
    convert_element_type x2 -> x0, other arithmetic: 3.78 us -> none  [the longest x1 3.67 us: body(): scaled = (shaped * (4.0 / points_total) / denominators[:, None, :]).resha...]
    dot_general x2 -> x1, matrix products: 5.77 us -> 5.36 us  [contract_rows(): lax.dot_general(left, right, (((0,), (0,)), ((), ())), preferred_element_...]
  transfers between devices with their start and end apart: 2 -> 0, of which waited for: 2 -> 0; matrix products, arithmetic and copies ran while one was open for 0% -> 0% of each run, Pallas kernels for 0% -> 0%
where the time goes in v1:
time: 115 us
  Pallas kernels  91.1 us (79%)
  matrix products  11 us (10%)
  other arithmetic  7.56 us (7%)
  local copies, waits for them, and re-layouts  4.31 us (4%)
    pallas_call x1, Pallas kernels, body(): pl.pallas_call(functools.partial(couple_kernel, n, orders), out_shape=jax...  56.7 us
    pallas_call x1, Pallas kernels, body(): pl.pallas_call(functools.partial(project_kernel, n), out_shape=(jax.Shape...  34.4 us
    dot_general x1, matrix products, body(): lax.dot_general(conduction, scaled, (((1,), (1,)), ((), ())), preferred_e...  5.6 us
    dot_general x1, matrix products, contract_rows(): lax.dot_general(left, right, (((0,), (0,)), ((), ())), preferred_element_...  5.36 us

profile of v1, /device:TPU:0, one launch (start us, length us, event | category | flops | bytes accessed | tf_op | source)
XLA Modules:
  0.0 114.6 jit_solution(10207219783708682494)
XLA Ops:
  0.6 0.0 copy-start
  0.6 1.5 %subtract_divide_fusion.weight_ref = f32[48,512]{1,0:T(8,128)} fusion(f32[512]{0:T(512)} %param.11, f32[48]{0:T(128)} %param.10), kind=kLoop, calls=%fused_computation.2 | loop fusion | flops 49152 | bytes 100544 | tf_op jit(solution)/shard_map/div | solution.py:256
  2.1 0.9 convert_element_type.14
  3.1 0.9 convert_element_type.13
  4.0 2.1 %multiply_convert_fusion = bf16[1024,64,48]{0,2,1:T(8,128)(2,1)S(1)} fusion(f32[1024,48]{0,1:T(8,128)S(1)} %convert_element_type.14, f32[1024,64]{0,1:T(8,128)S(1)} %convert_element_type.13), kind=kLoop, calls=%fused_computation.1 | loop fusion | flops 6291456 | bytes 6750208 | tf_op jit(solution)/shard_map/convert_element_type | solution.py:254
  6.1 0.0 copy-done
  6.1 5.4 %fusion.part_ref = f32[3072,512]{1,0:T(8,128)} fusion(bf16[1024,3072]{0,1:T(8,128)(2,1)S(1)} %bitcast.9, bf16[1024,512]{1,0:T(8,128)(2,1)S(1)} %copy-done), kind=kOutput, calls=%fused_computation.3 | convolution fusion | flops 3221225472 | bytes 13631488 | tf_op jit(solution)/shard_map/dot_general | solution.py:15
  11.5 56.7 %shard_map.77 = bf16[3072,512]{1,0:T(8,128)(2,1)} custom-call(f32[3072,512]{1,0:T(8,128)} %fusion.part_ref, f32[48,512]{1,0:T(8,128)} %subtract_divide_fusion.weight_ref), custom_call_target="tpu_custom_call" | custom-call | tf_op jit(solution)/shard_map/pallas_call | solution.py:262
  68.2 5.6 %fusion.1 = f32[3072,1024]{1,0:T(8,128)S(1)} fusion(bf16[3072,512]{1,0:T(8,128)(2,1)} %shard_map.77, bf16[1024,512]{1,0:T(8,128)(2,1)S(1)} %copy-done), kind=kOutput, calls=%fused_computation.4 | convolution fusion | flops 3221225472 | bytes 16777216 | tf_op jit(solution)/shard_map/dot_general | solution.py:279
  73.8 2.1 %multiply_reduce_fusion = f32[1024,64]{0,1:T(8,128)S(1)} fusion(f32[1024,64,48]{0,2,1:T(8,128)S(1)} %bitcast.8, f32[1024,48]{0,1:T(8,128)S(1)} %convert_element_type.14), kind=kLoop, calls=%fused_computation | loop fusion | flops 6225920 | bytes 13041664 | tf_op jit(solution)/shard_map/reduce_sum | solution.py:282
  75.9 1.0 copy.9.response_ref
  76.9 34.4 %shard_map.78 = (f32[64,64]{1,0:T(8,128)}, f32[1024,64]{1,0:T(8,128)}) custom-call(bf16[1024,1024]{1,0:T(8,128)(2,1)} %eigen_ref.1, f32[1024,64]{1,0:T(8,128)} %copy.9.response_ref), custom_call_target="tpu_custom_call" | custom-call | tf_op jit(solution)/shard_map/pallas_call | solution.py:288
  111.3 1.9 %copy.10 = f32[1024,64]{0,1:T(8,128)} copy(f32[1024,64]{1,0:T(8,128)} %get-tuple-element.5) | data formatting | bytes 524288 | tf_op jit(solution)/shard_map/pallas_call | solution.py:288
  113.2 1.4 %copy.12 = f32[64,64]{1,0:T(8,128)} copy(f32[64,64]{1,0:T(8,128)} %get-tuple-element.8) | data formatting | bytes 32768
Async XLA Ops:
  0.6 5.5 %copy-start = (bf16[1024,512]{1,0:T(8,128)(2,1)S(1)}, bf16[1024,512]{1,0:T(8,128)(2,1)}, u32[]{:S(2)}) copy-start(bf16[1024,512]{1,0:T(8,128)(2,1)} %param.7) | copy-start | bytes 3145732

commit v2 on v1

v2 whole, which is shorter than its diff:
```python
import functools

import jax
import jax.numpy as jnp
from jax import lax
from jax.experimental import pallas as pl
from jax.experimental.pallas import tpu as pltpu
from jax.sharding import PartitionSpec as P

MESH = pl.DeviceIdType.MESH
VMEM_BYTES = 56 * 1024 * 1024


def contract_rows(left, right):
    return lax.dot_general(
        left, right, (((0,), (0,)), ((), ())), preferred_element_type=jnp.float32
    )


def bit_of(me, bit):
    return lax.rem(lax.div(me, 1 << bit), 2)


def partner_of(me, bit):
    return me + (1 - 2 * bit_of(me, bit)) * (1 << bit)


def aligned(row, step):
    return pl.multiple_of(row, step)


def couple_kernel(
    n, orders, pairs_ref, conduction_ref, valence_ref, weight_ref, response_ref,
    scaled, acc, sent, got, send_sem, recv_sem,
):
    levels = n.bit_length() - 1
    me = lax.axis_index("grid")
    rows, columns = scaled.shape
    unit = weight_ref.shape[0]
    block = rows // n
    width = columns // len(orders)

    barrier = pltpu.get_barrier_semaphore()
    for bit in range(levels):
        pl.semaphore_signal(
            barrier, inc=1, device_id={"grid": partner_of(me, bit)}, device_id_type=MESH
        )
    pl.semaphore_wait(barrier, levels)

    slots = [rows - (rows >> s) for s in range(levels)]
    bases = [[0] for _ in orders]
    copies = [[] for _ in orders]

    def start_halving(q, s):
        size = (n >> (s + 1)) * block
        cols = pl.ds(q * width, width)
        copy = pltpu.make_async_remote_copy(
            src_ref=sent.at[pl.ds(slots[s], size), cols],
            dst_ref=got.at[pl.ds(slots[s], size), cols],
            send_sem=send_sem.at[q, s],
            recv_sem=recv_sem.at[q, s],
            device_id={"grid": partner_of(me, orders[q][s])},
            device_id_type=MESH,
        )
        copy.start()
        copies[q].append(copy)

    strip = 2 * width
    tile = rows // 8
    first = bit_of(me, 0)
    leave, keep = (1 - first) * (rows // 2), first * (rows // 2)
    for h in range(columns // strip):
        strip_cols = pl.ds(h * strip, strip)

        def product(row, strip_cols=strip_cols):
            return jnp.dot(
                pairs_ref[pl.ds(aligned(row, tile), tile), :],
                conduction_ref[:, strip_cols],
                preferred_element_type=jnp.float32,
            )

        def send_tile(i, _, product=product, strip_cols=strip_cols):
            sent[pl.ds(aligned(i * tile, tile), tile), strip_cols] = product(
                leave + i * tile
            ).astype(jnp.bfloat16)
            return 0

        def keep_tile(i, _, product=product, strip_cols=strip_cols):
            acc[pl.ds(aligned(keep + i * tile, tile), tile), strip_cols] = product(keep + i * tile)
            return 0

        lax.fori_loop(0, 4, send_tile, 0)
        start_halving(2 * h, 0)
        start_halving(2 * h + 1, 0)
        lax.fori_loop(0, 4, keep_tile, 0)
    for q in range(len(orders)):
        bases[q].append(first * (n // 2))

    for s in range(1, levels + 1):
        for q, order in enumerate(orders):
            cols = pl.ds(q * width, width)
            base = bases[q][s]
            copies[q][s - 1].wait_recv()

            def term(row, offset, s=s, cols=cols):
                return acc[pl.ds(aligned(row + offset, unit), unit), cols] + got[
                    pl.ds(aligned(slots[s - 1] + offset, unit), unit), cols
                ].astype(jnp.float32)

            if s == levels:
                def finish(i, _, term=term, base=base, cols=cols):
                    value = term(base * block, i * unit) * weight_ref[:, cols]
                    scaled[pl.ds(aligned(base * block + i * unit, unit), unit), cols] = (
                        value.astype(jnp.bfloat16)
                    )
                    return 0

                lax.fori_loop(0, block // unit, finish, 0)
                continue
            half = n >> (s + 1)
            bit = bit_of(me, order[s])
            give, hold = (1 - bit) * half * block, bit * half * block

            def pack(i, _, term=term, base=base, give=give, s=s, cols=cols):
                sent[pl.ds(aligned(slots[s] + i * unit, unit), unit), cols] = term(
                    base * block, give + i * unit
                ).astype(jnp.bfloat16)
                return 0

            def add(i, _, term=term, base=base, hold=hold, cols=cols):
                acc[pl.ds(aligned(base * block + hold + i * unit, unit), unit), cols] = term(
                    base * block, hold + i * unit
                )
                return 0

            lax.fori_loop(0, half * block // unit, pack, 0)
            start_halving(q, s)
            lax.fori_loop(0, half * block // unit, add, 0)
            bases[q].append(base + bit * half)

    for s in reversed(range(levels)):
        for q, order in enumerate(orders):
            if s < levels - 1:
                copies[q][-1].wait_recv()
            size = (n >> (s + 1)) * block
            view = scaled.at[
                pl.ds(aligned(bases[q][s + 1] * block, unit), size), pl.ds(q * width, width)
            ]
            copy = pltpu.make_async_remote_copy(
                src_ref=view,
                dst_ref=view,
                send_sem=send_sem.at[q, 2 * levels - 1 - s],
                recv_sem=recv_sem.at[q, 2 * levels - 1 - s],
                device_id={"grid": partner_of(me, order[s])},
                device_id_type=MESH,
            )
            copy.start()
            copies[q].append(copy)

    group = 8

    def respond(row):
        combined = lax.dot_general(
            scaled[pl.ds(aligned(row * unit, group * unit), group * unit), :],
            conduction_ref[...],
            (((1,), (1,)), ((), ())),
            preferred_element_type=jnp.float32,
        )
        weighted = combined.reshape(group, unit, combined.shape[1]) * valence_ref[...][None]
        response_ref[pl.ds(aligned(row, group), group), :] = jnp.sum(weighted, axis=1)

    potentials = rows // unit
    for position, start in enumerate((first, 1 - first)):
        if position:
            for q in range(len(orders)):
                copies[q][-1].wait_recv()

        def step(i, _, start=start):
            respond(start * (potentials // 2) + i * group)
            return 0

        lax.fori_loop(0, potentials // 2 // group, step, 0)
    for q in range(len(orders)):
        for copy in copies[q]:
            copy.wait_send()


def phases_of(n):
    phases, weight = [], 1
    while weight < n:
        radix = min(4, n // weight)
        phases.append((weight, radix))
        weight *= radix
    return phases


def place_of(block, n):
    place, size = 0, n
    for weight, radix in phases_of(n):
        size //= radix
        place += (block // weight % radix) * size
    return place


def project_kernel(
    n, eigen_ref, response_ref, projected_ref, remainder_ref, total_ref,
    acc, got, gathered, low, sums, send_sem, recv_sem, sum_send, sum_recv,
):
    me = lax.axis_index("grid")
    points, eigens = eigen_ref.shape
    count = response_ref.shape[0]
    block = eigens // n
    packed = block // 2
    phases = phases_of(n)

    barrier = pltpu.get_barrier_semaphore()
    for offset in range(1, n):
        pl.semaphore_signal(
            barrier, inc=1, device_id={"grid": lax.rem(me + offset, n)}, device_id_type=MESH
        )

    response_low = response_ref[...].astype(jnp.bfloat16)
    strip = min(256, eigens)
    for start in range(0, eigens, strip):
        part = jnp.dot(
            response_low, eigen_ref[:, start:start + strip], preferred_element_type=jnp.float32
        ).T
        for b in range(strip // block):
            place = place_of(start // block + b, n) * packed
            for side in range(2):
                row = b * block + side * packed
                acc[place:place + packed, side * count:(side + 1) * count] = part[row:row + packed, :]
    pl.semaphore_wait(barrier, n - 1)

    def peer(weight, radix, digit, offset):
        other = lax.rem(digit + offset, radix)
        return other, me + (other - digit) * weight

    copies = []
    bases = [0]
    slot = 0
    size = n
    index = 0
    for weight, radix in phases:
        size //= radix
        height = size * packed
        digit = lax.rem(lax.div(me, weight), radix)
        arriving = []
        for offset in range(1, radix):
            other, device = peer(weight, radix, digit, offset)
            copy = pltpu.make_async_remote_copy(
                src_ref=acc.at[pl.ds(aligned((bases[-1] + other * size) * packed, packed), height)],
                dst_ref=got.at[pl.ds(slot, height)],
                send_sem=send_sem.at[index],
                recv_sem=recv_sem.at[index],
                device_id={"grid": device},
                device_id_type=MESH,
            )
            copy.start()
            arriving.append((copy, slot))
            slot += height
            index += 1
        bases.append(bases[-1] + digit * size)
        kept = pl.ds(aligned(bases[-1] * packed, packed), height)
        value = acc[kept, :]
        for copy, place in arriving:
            copy.wait_recv()
            value = value + got[place:place + height, :]
            copies.append(copy)
        acc[kept, :] = value

    own = acc[pl.ds(aligned(bases[-1] * packed, packed), packed), :]
    mine = jnp.concatenate([own[:, :count], own[:, count:]], axis=0)
    gathered[pl.ds(aligned(bases[-1] * block, block), block), :] = mine.astype(jnp.bfloat16)
    for level in reversed(range(len(phases))):
        weight, radix = phases[level]
        digit = lax.rem(lax.div(me, weight), radix)
        height = size * block
        view = gathered.at[pl.ds(aligned(bases[level + 1] * block, block), height)]
        arriving = []
        for offset in range(1, radix):
            _, device = peer(weight, radix, digit, offset)
            copy = pltpu.make_async_remote_copy(
                src_ref=view,
                dst_ref=view,
                send_sem=send_sem.at[index],
                recv_sem=recv_sem.at[index],
                device_id={"grid": device},
                device_id_type=MESH,
            )
            copy.start()
            copies.append(copy)
            other, device = peer(weight, radix, digit, radix - offset)
            place = gathered.at[pl.ds(aligned((bases[level] + other * size) * block, block), height)]
            arriving.append(pltpu.make_async_remote_copy(
                src_ref=place,
                dst_ref=place,
                send_sem=send_sem.at[index],
                recv_sem=recv_sem.at[index],
                device_id={"grid": device},
                device_id_type=MESH,
            ))
            index += 1
        for copy in arriving:
            copy.wait_recv()
        size *= radix
    for b in range(n):
        place = place_of(b, n) * block
        low[b * block:(b + 1) * block, :] = gathered[place:place + block, :]

    wide = low[...].astype(jnp.float32)
    remainder = response_ref[...] - lax.dot_general(
        wide.T.astype(jnp.bfloat16), eigen_ref[...], (((1,), (1,)), ((), ())),
        preferred_element_type=jnp.float32,
    )
    squared = remainder * remainder
    lanes = squared[:, :128]
    for start in range(128, points, 128):
        lanes = lanes + squared[:, start:start + 128]
    sums[me] = jnp.broadcast_to(
        jnp.sum(lanes.T, axis=0, keepdims=True), sums.shape[1:]
    )
    for offset in range(1, n):
        copy = pltpu.make_async_remote_copy(
            src_ref=sums.at[me],
            dst_ref=sums.at[me],
            send_sem=sum_send.at[offset],
            recv_sem=sum_recv.at[offset],
            device_id={"grid": lax.rem(me + offset, n)},
            device_id_type=MESH,
        )
        copy.start()
        copies.append(copy)
    remainder_ref[...] = remainder
    squares = jnp.sum(wide * wide, axis=0, keepdims=True)
    projected_ref[...] = mine / jnp.sqrt(squares / eigens + 1e-06)
    for offset in range(1, n):
        other = lax.rem(me + n - offset, n)
        pltpu.make_async_remote_copy(
            src_ref=sums.at[other],
            dst_ref=sums.at[other],
            send_sem=sum_send.at[offset],
            recv_sem=sum_recv.at[offset],
            device_id={"grid": other},
            device_id_type=MESH,
        ).wait_recv()
    total_ref[...] = jnp.sum(sums[...], axis=0)
    for copy in copies:
        copy.wait_send()


def body(valence, conduction, potentials, eigenpotentials, valence_energy, conduction_energy):
    grid_rows = valence.shape[0]
    valence_count = valence.shape[1]
    conduction_count = conduction.shape[1]
    potential_count = potentials.shape[1]
    eigen_count = eigenpotentials.shape[1]
    n = lax.axis_size("grid")
    levels = n.bit_length() - 1
    points_total = grid_rows * n
    pair_count = potential_count * valence_count
    vmem = pl.BlockSpec(memory_space=pltpu.VMEM)

    valence_wide = valence.T.astype(jnp.float32)
    joined = potentials.T.astype(jnp.float32)[:, None, :] * valence_wide[None, :, :]
    pairs = joined.reshape(pair_count, grid_rows).astype(jnp.bfloat16)
    weight = (4.0 / points_total) / (valence_energy[:, None] - conduction_energy[None, :])

    plain = list(range(levels))
    crossed = [0, 2, 1] + plain[3:] if levels >= 3 else plain
    orders = [plain, crossed] * (conduction_count // 256)
    shape = (pair_count, conduction_count)
    response = pl.pallas_call(
        functools.partial(couple_kernel, n, orders),
        out_shape=jax.ShapeDtypeStruct((potential_count, grid_rows), jnp.float32),
        in_specs=[vmem] * 4,
        out_specs=vmem,
        scratch_shapes=[
            pltpu.VMEM(shape, jnp.bfloat16),
            pltpu.VMEM(shape, jnp.float32),
            pltpu.VMEM(shape, jnp.bfloat16),
            pltpu.VMEM(shape, jnp.bfloat16),
            pltpu.SemaphoreType.DMA((len(orders), 2 * levels)),
            pltpu.SemaphoreType.DMA((len(orders), 2 * levels)),
        ],
        compiler_params=pltpu.CompilerParams(
            collective_id=0, has_side_effects=True, vmem_limit_bytes=VMEM_BYTES
        ),
    )(pairs, conduction, valence_wide, weight)

    transfers = 2 * sum(radix - 1 for _, radix in phases_of(n))
    projected, remainder, total = pl.pallas_call(
        functools.partial(project_kernel, n),
        out_shape=(
            jax.ShapeDtypeStruct((eigen_count // n, potential_count), jnp.float32),
            jax.ShapeDtypeStruct((potential_count, grid_rows), jnp.float32),
            jax.ShapeDtypeStruct((8, potential_count), jnp.float32),
        ),
        in_specs=[vmem] * 2,
        out_specs=(vmem, vmem, vmem),
        scratch_shapes=[
            pltpu.VMEM((eigen_count // 2, 2 * potential_count), jnp.float32),
            pltpu.VMEM((eigen_count // 2, 2 * potential_count), jnp.float32),
            pltpu.VMEM((eigen_count, potential_count), jnp.bfloat16),
            pltpu.VMEM((eigen_count, potential_count), jnp.bfloat16),
            pltpu.VMEM((n, 8, potential_count), jnp.float32),
            pltpu.SemaphoreType.DMA((transfers,)),
            pltpu.SemaphoreType.DMA((transfers,)),
            pltpu.SemaphoreType.DMA((n,)),
            pltpu.SemaphoreType.DMA((n,)),
        ],
        compiler_params=pltpu.CompilerParams(
            collective_id=1, has_side_effects=True, vmem_limit_bytes=VMEM_BYTES
        ),
    )(eigenpotentials, response)
    root = jnp.sqrt(total[0] / points_total + 1e-06)
    return projected, (remainder / root[:, None]).T


def solution(mesh):
    return jax.shard_map(
        body,
        mesh=mesh,
        in_specs=(
            P(("grp", "grid"), None),
            P(("grp", "grid"), None),
            P(("grp", "grid"), None),
            P(("grp", "grid"), None),
            P("grp"),
            P("grp"),
        ),
        out_specs=(P(("grp", "grid"), None), P(("grp", "grid"), None)),
        check_vma=False,
    )
```

time: 115 us -> 100 us (0.87)
  matrix products: 11 us -> 0 us
  Pallas kernels: 91.1 us -> 87.4 us
  other arithmetic: 7.56 us -> 10.6 us
  local copies, waits for them, and re-layouts: 4.31 us -> 1.38 us
    dot_general x2 -> x0, matrix products: 11 us -> none  [the longest x1 5.6 us: body(): lax.dot_general(conduction, scaled, (((1,), (1,)), ((), ())), preferred_e...]
    pallas_call x1, Pallas kernels: 34.4 us -> 25.2 us  [body(): pl.pallas_call(functools.partial(project_kernel, n), out_shape=(jax.Shape...]
    pallas_call x1, Pallas kernels: 56.7 us -> 62.3 us  [body(): pl.pallas_call(functools.partial(couple_kernel, n, orders), out_shape=jax...]
    convert_element_type x3, other arithmetic: 3.96 us -> 6.72 us  [the longest x1 4.82 us: body(): pairs = joined.reshape(pair_count, grid_rows).astype(jnp.bfloat16)]
    reduce_sum x1 -> x0, other arithmetic: 2.1 us -> none  [body(): jnp.sum(combined.reshape(grid_rows, potential_count, valence_count) * val...]
    pallas_call x1 -> x0, local copies, waits for them, and re-layouts: 1.93 us -> none  [body(): pl.pallas_call(functools.partial(project_kernel, n), out_shape=(jax.Shape...]
    transpose x0 -> x1, other arithmetic: none -> 1.75 us  [body(): return (projected, (remainder / root[:, None]).T)]
where the time goes in v2:
time: 100 us
  Pallas kernels  87.4 us (87%)
  other arithmetic  10.6 us (11%)
  local copies, waits for them, and re-layouts  1.38 us (1%)
    pallas_call x1, Pallas kernels, body(): pl.pallas_call(functools.partial(couple_kernel, n, orders), out_shape=jax...  62.3 us
    pallas_call x1, Pallas kernels, body(): pl.pallas_call(functools.partial(project_kernel, n), out_shape=(jax.Shape...  25.2 us
    convert_element_type x1, other arithmetic, body(): pairs = joined.reshape(pair_count, grid_rows).astype(jnp.bfloat16)  4.82 us

profile of v2, /device:TPU:0, one launch (start us, length us, event | category | flops | bytes accessed | tf_op | source)
XLA Modules:
  0.0 100.0 jit_solution(5739604618050851253)
XLA Ops:
  0.6 1.4 %subtract_divide_fusion.weight_ref = f32[48,512]{1,0:T(8,128)} fusion(f32[512]{0:T(512)} %param.11, f32[48]{0:T(128)} %param.10), kind=kLoop, calls=%fused_computation.4 | loop fusion | flops 49152 | bytes 100544 | tf_op jit(solution)/shard_map/div | solution.py:367
  2.0 0.9 convert_bitcast_fusion.1.valence_ref
  3.0 0.0 copy-start
  3.0 1.0 convert_bitcast_fusion
  4.0 4.8 %multiply_convert_fusion = bf16[64,48,1024]{2,1,0:T(8,128)(2,1)} fusion(f32[48,1024]{1,0:T(8,128)S(1)} %convert_bitcast_fusion.1.valence_ref, f32[64,1024]{1,0:T(8,128)S(1)} %convert_bitcast_fusion), kind=kLoop, calls=%fused_computation | loop fusion | flops 6291456 | bytes 6750208 | tf_op jit(solution)/shard_map/convert_element_type | solution.py:366
  8.8 0.0 copy-done
  8.8 62.3 %shard_map.77.response_ref = f32[64,1024]{1,0:T(8,128)} custom-call(bf16[3072,1024]{1,0:T(8,128)(2,1)} %bitcast.9, bf16[1024,512]{1,0:T(8,128)(2,1)} %conduction_ref.1, f32[48,1024]{1,0:T(8,128)} %copy-done, f32[48,512]{1,0:T(8,128)} %subtract_divide_fusion.weight_ref), custom_call_target="tpu_custom_call" | custom-call | tf_op jit(solution)/shard_map/pallas_call | solution.py:373
  71.1 25.2 %shard_map.78 = (f32[64,64]{1,0:T(8,128)}, f32[64,1024]{1,0:T(8,128)}, f32[8,64]{1,0:T(8,128)}) custom-call(bf16[1024,1024]{1,0:T(8,128)(2,1)} %eigen_ref.1, f32[64,1024]{1,0:T(8,128)} %shard_map.77.response_ref), custom_call_target="tpu_custom_call" | custom-call | tf_op jit(solution)/shard_map/pallas_call | solution.py:392
  96.2 0.7 sqrt_bitcast_fusion
  96.9 1.7 %divide_bitcast_fusion = f32[1024,64]{0,1:T(8,128)} fusion(f32[64,1024]{1,0:T(8,128)} %get-tuple-element.6, f32[64]{0:T(128)S(1)} %sqrt_bitcast_fusion), kind=kLoop, calls=%fused_computation.2 | loop fusion | flops 65536 | bytes 524544 | tf_op jit(solution)/shard_map/transpose | solution.py:417
  98.7 1.4 %copy.9 = f32[64,64]{1,0:T(8,128)} copy(f32[64,64]{1,0:T(8,128)} %get-tuple-element.10) | data formatting | bytes 32768
Async XLA Ops:
  3.0 5.8 %copy-start = (f32[48,1024]{1,0:T(8,128)}, f32[48,1024]{1,0:T(8,128)S(1)}, u32[]{:S(2)}) copy-start(f32[48,1024]{1,0:T(8,128)S(1)} %convert_bitcast_fusion.1.valence_ref) | copy-start | bytes 589828

commit v3 on v2

--- a/solution.py
+++ b/solution.py
@@ -30,13 +30,14 @@
 
 
 def couple_kernel(
-    n, orders, pairs_ref, conduction_ref, valence_ref, weight_ref, response_ref,
-    scaled, acc, sent, got, send_sem, recv_sem,
+    n, orders, lags, valence_ref, conduction_ref, potential_ref, filled_ref, empty_ref, response_ref,
+    wide, weight, scaled, acc, sent, got, send_sem, recv_sem,
 ):
     levels = n.bit_length() - 1
     me = lax.axis_index("grid")
     rows, columns = scaled.shape
-    unit = weight_ref.shape[0]
+    unit = valence_ref.shape[0]
+    points = valence_ref.shape[1] * n
     block = rows // n
     width = columns // len(orders)
 
@@ -45,7 +46,9 @@
         pl.semaphore_signal(
             barrier, inc=1, device_id={"grid": partner_of(me, bit)}, device_id_type=MESH
         )
-    pl.semaphore_wait(barrier, levels)
+    wide[...] = valence_ref[...].astype(jnp.float32)
+    energies = jnp.broadcast_to(filled_ref[...], (8, unit)).T[:, 0:1]
+    weight[...] = (4.0 / points) / (energies - empty_ref[...])
 
     slots = [rows - (rows >> s) for s in range(levels)]
     bases = [[0] for _ in orders]
@@ -65,99 +68,107 @@
         copy.start()
         copies[q].append(copy)
 
-    strip = 2 * width
-    tile = rows // 8
+    group = 8
+    tile = group * unit
+    tiles = rows // tile // 2
     first = bit_of(me, 0)
-    leave, keep = (1 - first) * (rows // 2), first * (rows // 2)
-    for h in range(columns // strip):
-        strip_cols = pl.ds(h * strip, strip)
-
-        def product(row, strip_cols=strip_cols):
-            return jnp.dot(
-                pairs_ref[pl.ds(aligned(row, tile), tile), :],
-                conduction_ref[:, strip_cols],
-                preferred_element_type=jnp.float32,
-            )
-
-        def send_tile(i, _, product=product, strip_cols=strip_cols):
-            sent[pl.ds(aligned(i * tile, tile), tile), strip_cols] = product(
-                leave + i * tile
+
+    def product(index):
+        potential = potential_ref[pl.ds(aligned(index * group, group), group), :]
+        pairs = potential[:, None, :] * wide[...][None]
+        return jnp.dot(
+            pairs.reshape(tile, wide.shape[1]).astype(jnp.bfloat16),
+            conduction_ref[...],
+            preferred_element_type=jnp.float32,
+        )
+
+    def send_tile(i, _):
+        sent[pl.ds(aligned(i * tile, tile), tile), :] = product(
+            (1 - first) * tiles + i
+        ).astype(jnp.bfloat16)
+        return 0
+
+    def keep_tile(i, _):
+        index = first * tiles + i
+        acc[pl.ds(aligned(index * tile, tile), tile), :] = product(index)
+        return 0
+
+    lax.fori_loop(0, tiles, send_tile, 0)
+    pl.semaphore_wait(barrier, levels)
+    for q in range(len(orders)):
+        start_halving(q, 0)
+    lax.fori_loop(0, tiles, keep_tile, 0)
+    for q in range(len(orders)):
+        bases[q].append(first * (n // 2))
+
+    def halve(q, s):
+        order = orders[q]
+        cols = pl.ds(q * width, width)
+        base = bases[q][s]
+        copies[q][s - 1].wait_recv()
+
+        def term(row, offset):
+            return acc[pl.ds(aligned(row + offset, unit), unit), cols] + got[
+                pl.ds(aligned(slots[s - 1] + offset, unit), unit), cols
+            ].astype(jnp.float32)
+
+        if s == levels:
+            def finish(i, _):
+                value = term(base * block, i * unit) * weight[:, cols]
+                scaled[pl.ds(aligned(base * block + i * unit, unit), unit), cols] = (
+                    value.astype(jnp.bfloat16)
+                )
+                return 0
+
+            lax.fori_loop(0, block // unit, finish, 0)
+            return
+        half = n >> (s + 1)
+        bit = bit_of(me, order[s])
+        give, hold = (1 - bit) * half * block, bit * half * block
+
+        def pack(i, _):
+            sent[pl.ds(aligned(slots[s] + i * unit, unit), unit), cols] = term(
+                base * block, give + i * unit
             ).astype(jnp.bfloat16)
             return 0
 
-        def keep_tile(i, _, product=product, strip_cols=strip_cols):
-            acc[pl.ds(aligned(keep + i * tile, tile), tile), strip_cols] = product(keep + i * tile)
+        def add(i, _):
+            acc[pl.ds(aligned(base * block + hold + i * unit, unit), unit), cols] = term(
+                base * block, hold + i * unit
+            )
             return 0
 
-        lax.fori_loop(0, 4, send_tile, 0)
-        start_halving(2 * h, 0)
-        start_halving(2 * h + 1, 0)
-        lax.fori_loop(0, 4, keep_tile, 0)
-    for q in range(len(orders)):
-        bases[q].append(first * (n // 2))
-
-    for s in range(1, levels + 1):
-        for q, order in enumerate(orders):
-            cols = pl.ds(q * width, width)
-            base = bases[q][s]
-            copies[q][s - 1].wait_recv()
-
-            def term(row, offset, s=s, cols=cols):
-                return acc[pl.ds(aligned(row + offset, unit), unit), cols] + got[
-                    pl.ds(aligned(slots[s - 1] + offset, unit), unit), cols
-                ].astype(jnp.float32)
-
-            if s == levels:
-                def finish(i, _, term=term, base=base, cols=cols):
-                    value = term(base * block, i * unit) * weight_ref[:, cols]
-                    scaled[pl.ds(aligned(base * block + i * unit, unit), unit), cols] = (
-                        value.astype(jnp.bfloat16)
-                    )
-                    return 0
-
-                lax.fori_loop(0, block // unit, finish, 0)
-                continue
-            half = n >> (s + 1)
-            bit = bit_of(me, order[s])
-            give, hold = (1 - bit) * half * block, bit * half * block
-
-            def pack(i, _, term=term, base=base, give=give, s=s, cols=cols):
-                sent[pl.ds(aligned(slots[s] + i * unit, unit), unit), cols] = term(
-                    base * block, give + i * unit
-                ).astype(jnp.bfloat16)
-                return 0
-
-            def add(i, _, term=term, base=base, hold=hold, cols=cols):
-                acc[pl.ds(aligned(base * block + hold + i * unit, unit), unit), cols] = term(
-                    base * block, hold + i * unit
-                )
-                return 0
-
-            lax.fori_loop(0, half * block // unit, pack, 0)
-            start_halving(q, s)
-            lax.fori_loop(0, half * block // unit, add, 0)
-            bases[q].append(base + bit * half)
-
-    for s in reversed(range(levels)):
-        for q, order in enumerate(orders):
-            if s < levels - 1:
-                copies[q][-1].wait_recv()
-            size = (n >> (s + 1)) * block
-            view = scaled.at[
-                pl.ds(aligned(bases[q][s + 1] * block, unit), size), pl.ds(q * width, width)
-            ]
-            copy = pltpu.make_async_remote_copy(
-                src_ref=view,
-                dst_ref=view,
-                send_sem=send_sem.at[q, 2 * levels - 1 - s],
-                recv_sem=recv_sem.at[q, 2 * levels - 1 - s],
-                device_id={"grid": partner_of(me, order[s])},
-                device_id_type=MESH,
-            )
-            copy.start()
-            copies[q].append(copy)
-
-    group = 8
+        lax.fori_loop(0, half * block // unit, pack, 0)
+        start_halving(q, s)
+        lax.fori_loop(0, half * block // unit, add, 0)
+        bases[q].append(base + bit * half)
+
+    def double(q, s):
+        if s < levels - 1:
+            copies[q][-1].wait_recv()
+        size = (n >> (s + 1)) * block
+        view = scaled.at[
+            pl.ds(aligned(bases[q][s + 1] * block, unit), size), pl.ds(q * width, width)
+        ]
+        copy = pltpu.make_async_remote_copy(
+            src_ref=view,
+            dst_ref=view,
+            send_sem=send_sem.at[q, 2 * levels - 1 - s],
+            recv_sem=recv_sem.at[q, 2 * levels - 1 - s],
+            device_id={"grid": partner_of(me, orders[q][s])},
+            device_id_type=MESH,
+        )
+        copy.start()
+        copies[q].append(copy)
+
+    events = sorted(
+        (event + lags[q], q, event) for q in range(len(orders)) for event in range(1, 2 * levels)
+    )
+    for _, q, event in events:
+        if event <= levels:
+            halve(q, event)
+        if event >= levels:
+            double(q, 2 * levels - 1 - event)
 
     def respond(row):
         combined = lax.dot_general(
@@ -166,7 +177,7 @@
             (((1,), (1,)), ((), ())),
             preferred_element_type=jnp.float32,
         )
-        weighted = combined.reshape(group, unit, combined.shape[1]) * valence_ref[...][None]
+        weighted = combined.reshape(group, unit, combined.shape[1]) * wide[...][None]
         response_ref[pl.ds(aligned(row, group), group), :] = jnp.sum(weighted, axis=1)
 
     potentials = rows // unit
@@ -211,6 +222,7 @@
     count = response_ref.shape[0]
     block = eigens // n
     packed = block // 2
+    low_rows = gathered.shape[0] // n
     phases = phases_of(n)
 
     barrier = pltpu.get_barrier_semaphore()
@@ -271,12 +283,14 @@
 
     own = acc[pl.ds(aligned(bases[-1] * packed, packed), packed), :]
     mine = jnp.concatenate([own[:, :count], own[:, count:]], axis=0)
-    gathered[pl.ds(aligned(bases[-1] * block, block), block), :] = mine.astype(jnp.bfloat16)
+    gathered[pl.ds(aligned(bases[-1] * low_rows, low_rows), low_rows), :] = (
+        own if low_rows == packed else mine
+    ).astype(jnp.bfloat16)
     for level in reversed(range(len(phases))):
         weight, radix = phases[level]
         digit = lax.rem(lax.div(me, weight), radix)
-        height = size * block
-        view = gathered.at[pl.ds(aligned(bases[level + 1] * block, block), height)]
+        height = size * low_rows
+        view = gathered.at[pl.ds(aligned(bases[level + 1] * low_rows, low_rows), height)]
         arriving = []
         for offset in range(1, radix):
             _, device = peer(weight, radix, digit, offset)
@@ -291,7 +305,9 @@
             copy.start()
             copies.append(copy)
             other, device = peer(weight, radix, digit, radix - offset)
-            place = gathered.at[pl.ds(aligned((bases[level] + other * size) * block, block), height)]
+            place = gathered.at[
+                pl.ds(aligned((bases[level] + other * size) * low_rows, low_rows), height)
+            ]
             arriving.append(pltpu.make_async_remote_copy(
                 src_ref=place,
                 dst_ref=place,
@@ -305,8 +321,12 @@
             copy.wait_recv()
         size *= radix
     for b in range(n):
-        place = place_of(b, n) * block
-        low[b * block:(b + 1) * block, :] = gathered[place:place + block, :]
+        place = place_of(b, n) * low_rows
+        for part in range(block // low_rows):
+            row = b * block + part * low_rows
+            low[row:row + low_rows, :] = gathered[
+                place:place + low_rows, part * count:(part + 1) * count
+            ]
 
     wide = low[...].astype(jnp.float32)
     remainder = response_ref[...] - lax.dot_general(
@@ -361,21 +381,20 @@
     pair_count = potential_count * valence_count
     vmem = pl.BlockSpec(memory_space=pltpu.VMEM)
 
-    valence_wide = valence.T.astype(jnp.float32)
-    joined = potentials.T.astype(jnp.float32)[:, None, :] * valence_wide[None, :, :]
-    pairs = joined.reshape(pair_count, grid_rows).astype(jnp.bfloat16)
-    weight = (4.0 / points_total) / (valence_energy[:, None] - conduction_energy[None, :])
-
     plain = list(range(levels))
     crossed = [0, 2, 1] + plain[3:] if levels >= 3 else plain
-    orders = [plain, crossed] * (conduction_count // 256)
+    chunks = conduction_count // 128
+    orders = [crossed if q % 4 == 3 else plain for q in range(chunks)]
+    lags = [1 if q % 4 == 1 else 0 for q in range(chunks)]
     shape = (pair_count, conduction_count)
     response = pl.pallas_call(
-        functools.partial(couple_kernel, n, orders),
+        functools.partial(couple_kernel, n, orders, lags),
         out_shape=jax.ShapeDtypeStruct((potential_count, grid_rows), jnp.float32),
-        in_specs=[vmem] * 4,
+        in_specs=[vmem] * 5,
         out_specs=vmem,
         scratch_shapes=[
+            pltpu.VMEM((valence_count, grid_rows), jnp.float32),
+            pltpu.VMEM((valence_count, conduction_count), jnp.float32),
             pltpu.VMEM(shape, jnp.bfloat16),
             pltpu.VMEM(shape, jnp.float32),
             pltpu.VMEM(shape, jnp.bfloat16),
@@ -386,8 +405,12 @@
         compiler_params=pltpu.CompilerParams(
             collective_id=0, has_side_effects=True, vmem_limit_bytes=VMEM_BYTES
         ),
-    )(pairs, conduction, valence_wide, weight)
-
+    )(
+        valence.T, conduction, potentials.T.astype(jnp.float32),
+        valence_energy[None, :], conduction_energy[None, :],
+    )
+
+    fold = 2 if eigen_count // n % 32 == 0 else 1
     transfers = 2 * sum(radix - 1 for _, radix in phases_of(n))
     projected, remainder, total = pl.pallas_call(
         functools.partial(project_kernel, n),
@@ -401,7 +424,7 @@
         scratch_shapes=[
             pltpu.VMEM((eigen_count // 2, 2 * potential_count), jnp.float32),
             pltpu.VMEM((eigen_count // 2, 2 * potential_count), jnp.float32),
-            pltpu.VMEM((eigen_count, potential_count), jnp.bfloat16),
+            pltpu.VMEM((eigen_count // fold, fold * potential_count), jnp.bfloat16),
             pltpu.VMEM((eigen_count, potential_count), jnp.bfloat16),
             pltpu.VMEM((n, 8, potential_count), jnp.float32),
             pltpu.SemaphoreType.DMA((transfers,)),

time: 100 us -> 92.9 us (0.929)
  other arithmetic: 10.6 us -> 4.05 us
    convert_element_type x3 -> x1, other arithmetic: 6.72 us -> 1.63 us  [body(): potentials.T.astype(jnp.float32)]
    div x1 -> x0, other arithmetic: 1.41 us -> none  [body(): 4.0 / points_total / (valence_energy[:, None] - conduction_energy[None, :])]
where the time goes in v3:
time: 92.9 us; the launch traced here: 92.6 us
  Pallas kernels  86.5 us (93%)
  other arithmetic  4.05 us (4%)
  local copies, waits for them, and re-layouts  1.37 us (1%)
    pallas_call x1, Pallas kernels, body(): pl.pallas_call(functools.partial(couple_kernel, n, orders, lags), out_sha...  61.9 us
    pallas_call x1, Pallas kernels, body(): pl.pallas_call(functools.partial(project_kernel, n), out_shape=(jax.Shape...  24.6 us

profile of v3, /device:TPU:0, one launch (start us, length us, event | category | flops | bytes accessed | tf_op | source)
XLA Modules:
  0.0 92.6 jit_solution(7311879179853931587)
XLA Ops:
  0.6 1.6 %convert_bitcast_fusion.potential_ref = f32[64,1024]{1,0:T(8,128)} fusion(bf16[1024,64]{0,1:T(8,128)(2,1)} %param.8), kind=kLoop, calls=%fused_computation | loop fusion | flops 65536 | bytes 393216 | tf_op jit(solution)/shard_map/convert_element_type | solution.py:409
  2.3 61.9 %shard_map.77.response_ref = f32[64,1024]{1,0:T(8,128)} custom-call(bf16[48,1024]{1,0:T(8,128)(2,1)} %bitcast.9, bf16[1024,512]{1,0:T(8,128)(2,1)} %conduction_ref.1, f32[64,1024]{1,0:T(8,128)} %convert_bitcast_fusion.potential_ref, f32[1,48]{1,0:T(1,128)} %bitcast.11, f32[1,512]{1,0:T(1,128)} %bitcast.10), custom_call_target="tpu_custom_call" | custom-call | tf_op jit(solution)/shard_map/pallas_call | solution.py:390
  64.2 24.6 %shard_map.78 = (f32[64,64]{1,0:T(8,128)}, f32[64,1024]{1,0:T(8,128)}, f32[8,64]{1,0:T(8,128)}) custom-call(bf16[1024,1024]{1,0:T(8,128)(2,1)} %eigen_ref.1, f32[64,1024]{1,0:T(8,128)} %shard_map.77.response_ref), custom_call_target="tpu_custom_call" | custom-call | tf_op jit(solution)/shard_map/pallas_call | solution.py:415
  88.8 0.7 sqrt_bitcast_fusion
  89.5 1.7 %divide_bitcast_fusion = f32[1024,64]{0,1:T(8,128)} fusion(f32[64,1024]{1,0:T(8,128)} %get-tuple-element.6, f32[64]{0:T(128)S(1)} %sqrt_bitcast_fusion), kind=kLoop, calls=%fused_computation.1 | loop fusion | flops 65536 | bytes 524544 | tf_op jit(solution)/shard_map/transpose | solution.py:440
  91.2 1.4 %copy.9 = f32[64,64]{1,0:T(8,128)} copy(f32[64,64]{1,0:T(8,128)} %get-tuple-element.10) | data formatting | bytes 32768

commit v4 on v3

--- a/solution.py
+++ b/solution.py
@@ -31,7 +31,7 @@
 
 def couple_kernel(
     n, orders, lags, valence_ref, conduction_ref, potential_ref, filled_ref, empty_ref, response_ref,
-    wide, weight, scaled, acc, sent, got, send_sem, recv_sem,
+    wide, factor, weight, scaled, acc, sent, got, send_sem, recv_sem,
 ):
     levels = n.bit_length() - 1
     me = lax.axis_index("grid")
@@ -47,6 +47,7 @@
             barrier, inc=1, device_id={"grid": partner_of(me, bit)}, device_id_type=MESH
         )
     wide[...] = valence_ref[...].astype(jnp.float32)
+    factor[...] = potential_ref[...].astype(jnp.float32)
     energies = jnp.broadcast_to(filled_ref[...], (8, unit)).T[:, 0:1]
     weight[...] = (4.0 / points) / (energies - empty_ref[...])
 
@@ -74,7 +75,7 @@
     first = bit_of(me, 0)
 
     def product(index):
-        potential = potential_ref[pl.ds(aligned(index * group, group), group), :]
+        potential = factor[pl.ds(aligned(index * group, group), group), :]
         pairs = potential[:, None, :] * wide[...][None]
         return jnp.dot(
             pairs.reshape(tile, wide.shape[1]).astype(jnp.bfloat16),
@@ -214,7 +215,7 @@
 
 
 def project_kernel(
-    n, eigen_ref, response_ref, projected_ref, remainder_ref, total_ref,
+    n, eigen_ref, response_ref, projected_ref, complementary_ref,
     acc, got, gathered, low, sums, send_sem, recv_sem, sum_send, sum_recv,
 ):
     me = lax.axis_index("grid")
@@ -351,7 +352,7 @@
         )
         copy.start()
         copies.append(copy)
-    remainder_ref[...] = remainder
+    complementary_ref[...] = remainder
     squares = jnp.sum(wide * wide, axis=0, keepdims=True)
     projected_ref[...] = mine / jnp.sqrt(squares / eigens + 1e-06)
     for offset in range(1, n):
@@ -364,7 +365,8 @@
             device_id={"grid": other},
             device_id_type=MESH,
         ).wait_recv()
-    total_ref[...] = jnp.sum(sums[...], axis=0)
+    total = jnp.sum(sums[...], axis=0).T[:, 0:1]
+    complementary_ref[...] = complementary_ref[...] / jnp.sqrt(total / (points * n) + 1e-06)
     for copy in copies:
         copy.wait_send()
 
@@ -384,8 +386,8 @@
     plain = list(range(levels))
     crossed = [0, 2, 1] + plain[3:] if levels >= 3 else plain
     chunks = conduction_count // 128
-    orders = [crossed if q % 4 == 3 else plain for q in range(chunks)]
-    lags = [1 if q % 4 == 1 else 0 for q in range(chunks)]
+    orders = [crossed if q % 2 == 1 else plain for q in range(chunks)]
+    lags = [(0, 0, 1, 1)[q % 4] for q in range(chunks)]
     shape = (pair_count, conduction_count)
     response = pl.pallas_call(
         functools.partial(couple_kernel, n, orders, lags),
@@ -394,6 +396,7 @@
         out_specs=vmem,
         scratch_shapes=[
             pltpu.VMEM((valence_count, grid_rows), jnp.float32),
+            pltpu.VMEM((potential_count, grid_rows), jnp.float32),
             pltpu.VMEM((valence_count, conduction_count), jnp.float32),
             pltpu.VMEM(shape, jnp.bfloat16),
             pltpu.VMEM(shape, jnp.float32),
@@ -406,21 +409,20 @@
             collective_id=0, has_side_effects=True, vmem_limit_bytes=VMEM_BYTES
         ),
     )(
-        valence.T, conduction, potentials.T.astype(jnp.float32),
+        valence.T, conduction, potentials.T,
         valence_energy[None, :], conduction_energy[None, :],
     )
 
     fold = 2 if eigen_count // n % 32 == 0 else 1
     transfers = 2 * sum(radix - 1 for _, radix in phases_of(n))
-    projected, remainder, total = pl.pallas_call(
+    projected, complementary = pl.pallas_call(
         functools.partial(project_kernel, n),
         out_shape=(
             jax.ShapeDtypeStruct((eigen_count // n, potential_count), jnp.float32),
             jax.ShapeDtypeStruct((potential_count, grid_rows), jnp.float32),
-            jax.ShapeDtypeStruct((8, potential_count), jnp.float32),
         ),
         in_specs=[vmem] * 2,
-        out_specs=(vmem, vmem, vmem),
+        out_specs=(vmem, vmem),
         scratch_shapes=[
             pltpu.VMEM((eigen_count // 2, 2 * potential_count), jnp.float32),
             pltpu.VMEM((eigen_count // 2, 2 * potential_count), jnp.float32),
@@ -436,8 +438,7 @@
             collective_id=1, has_side_effects=True, vmem_limit_bytes=VMEM_BYTES
         ),
     )(eigenpotentials, response)
-    root = jnp.sqrt(total[0] / points_total + 1e-06)
-    return projected, (remainder / root[:, None]).T
+    return projected, complementary.T
 
 
 def solution(mesh):

time: 92.9 us -> 84.5 us (0.910)
  Pallas kernels: 86.5 us -> 80.6 us
  other arithmetic: 4.05 us -> 0 us
  local copies, waits for them, and re-layouts: 1.37 us -> 3.05 us
    pallas_call x1, Pallas kernels: 61.9 us -> 55.2 us  [body(): pl.pallas_call(functools.partial(couple_kernel, n, orders, lags), out_sha...]
    transpose x1 -> x0, other arithmetic: 1.75 us -> none  [body(): return (projected, (remainder / root[:, None]).T)]
    unnamed x1 -> x2, local copies, waits for them, and re-layouts: 1.37 us -> 3.05 us
    convert_element_type x1 -> x0, other arithmetic: 1.63 us -> none  [body(): potentials.T.astype(jnp.float32)]
where the time goes in v4:
time: 84.5 us; the launch traced here: 84.3 us
  Pallas kernels  80.6 us (95%)
  local copies, waits for them, and re-layouts  3.05 us (4%)
    pallas_call x1, Pallas kernels, body(): pl.pallas_call(functools.partial(couple_kernel, n, orders, lags), out_sha...  55.2 us
    pallas_call x1, Pallas kernels, body(): pl.pallas_call(functools.partial(project_kernel, n), out_shape=(jax.Shape...  25.3 us
    unnamed x2, local copies, waits for them, and re-layouts  3.05 us

profile of v4, /device:TPU:0, one launch (start us, length us, event | category | flops | bytes accessed | tf_op | source)
XLA Modules:
  0.0 84.3 jit_solution(17148120139988596298)
XLA Ops:
  0.6 55.2 %shard_map.77.response_ref = f32[64,1024]{1,0:T(8,128)} custom-call(bf16[48,1024]{1,0:T(8,128)(2,1)} %bitcast.7, bf16[1024,512]{1,0:T(8,128)(2,1)} %conduction_ref.1, bf16[64,1024]{1,0:T(8,128)(2,1)} %bitcast.6, f32[1,48]{1,0:T(1,128)} %bitcast.9, f32[1,512]{1,0:T(1,128)} %bitcast.8), custom_call_target="tpu_custom_call" | custom-call | tf_op jit(solution)/shard_map/pallas_call | solution.py:392
  55.9 25.3 %shard_map.78 = (f32[64,64]{1,0:T(8,128)}, f32[64,1024]{1,0:T(8,128)}) custom-call(bf16[1024,1024]{1,0:T(8,128)(2,1)} %eigen_ref.1, f32[64,1024]{1,0:T(8,128)} %shard_map.77.response_ref), custom_call_target="tpu_custom_call" | custom-call | tf_op jit(solution)/shard_map/pallas_call | solution.py:418
  81.2 1.4 %copy.10 = f32[64,64]{1,0:T(8,128)} copy(f32[64,64]{1,0:T(8,128)} %get-tuple-element.8) | data formatting | bytes 32768
  82.6 1.7 %copy.11 = f32[1024,64]{0,1:T(8,128)} copy(f32[1024,64]{0,1:T(8,128)} %bitcast.5) | data formatting | bytes 524288
